TPU v7x, 512 devices: a whole 4x8x8 slice. The times are simulated.
512 devices in a mesh: dp: 16 (over y, core), tensor: 32 (over z, x).
Axes of the slice: x: 4, y: 8, z: 8, core: 2. Of those that a mesh axis runs over, the one named last changes fastest.
Arguments:
- tokens: bfloat16 [2048, 4096], P('dp', 'tensor'), may hold values from -6 to 6
- gate_pre: bfloat16 [2048, 16384], P('dp', 'tensor'), may hold values from -6 to 6
- up_blocks: bfloat16 [32, 64, 128, 128], P('tensor'), may hold values from -0.125 to 0.125
- up_mask: int32 [32, 128], P(None, 'tensor'), may hold values from 0 to 1, as said below
- down_blocks: bfloat16 [32, 64, 128, 128], P('tensor'), may hold values from -0.0625 to 0.0625
- down_mask: int32 [128, 32], replicated, may hold values from 0 to 1, as said below
- down_owner: int32 [128], replicated, may hold values from 0 to 31, as said below
- cotangent: bfloat16 [2048, 4096], P('dp', 'tensor'), may hold values from -6 to 6
Outputs:
- mixed: bfloat16 [2048, 4096], P('dp', 'tensor')
- input_grad: bfloat16 [2048, 4096], P('dp', 'tensor')
- gate_grad: bfloat16 [2048, 16384], P('dp', 'tensor')
- up_grad: bfloat16 [32, 64, 128, 128], P('tensor', 'dp')
- down_grad: bfloat16 [32, 64, 128, 128], P('tensor', 'dp')
Inputs may be any that keep to these rules, and one draw needn't show every extreme that they name: `up_mask`: each column strip of 4 block columns holds exactly 64 ones. `down_mask`: the rows owned by one device hold exactly 64 ones together. `down_owner`: every device owns exactly 4 block rows.
All inputs are finite; a program needn't handle non-finite values.
Results may differ from a plain program's by a relative error of at most 0.022.
Values may be sent and summed in bfloat16 or wider, within the bound.
No kernel may reach another device: no remote copies, remote signals or barrier semaphores. Data moves between devices by JAX's collectives and lax.ppermute only.
A program may use at most 128 MiB of HBM per device.

v0:
```python
import jax
import jax.numpy as jnp
from jax import lax
from jax.sharding import PartitionSpec as P


def kept_positions(marked, total):
    marked = marked.reshape(-1).astype(jnp.int32)
    running = jnp.cumsum(marked) - 1
    target = jnp.where(marked > 0, running, total)
    indices = jnp.arange(marked.shape[0], dtype=jnp.int32)
    return jnp.zeros((total,), jnp.int32).at[target].set(indices, mode="drop")


def one_hot(indices, total):
    return (indices[:, None] == jnp.arange(total, dtype=jnp.int32)[None, :]).astype(jnp.float32)


def row_slots(down_owner, devices):
    marks = (down_owner[:, None] == jnp.arange(devices, dtype=jnp.int32)[None, :]).astype(jnp.int32)
    earlier = jnp.cumsum(marks, axis=0) - marks
    return jnp.sum(earlier * marks, axis=1)


def picker(wanted, block, current, segment):
    block_count = segment.shape[1] // block
    inside = (wanted >= 0) & (wanted < block_count)
    shaped = segment.reshape(segment.shape[0], block_count, block)
    chosen = jnp.take(shaped, jnp.clip(wanted, 0, block_count - 1), axis=1)
    return jnp.where(inside[None, :, None], chosen, current)


def shards(tokens, gate_pre, up_blocks, up_mask, down_blocks, down_mask, down_owner, cotangent):
    devices = lax.axis_size("tensor")
    position = lax.axis_index("tensor")
    token_count = tokens.shape[0]
    blocks_wide = up_mask.shape[0]
    strip_size = up_mask.shape[1]
    block = up_blocks.shape[2]
    kept_up = up_blocks.shape[1]
    kept_down = down_blocks.shape[1]
    model_width = blocks_wide * block
    highest = lax.Precision.HIGHEST
    x_full, dy_full = (
        lax.all_gather(tokens, "tensor", axis=1, tiled=True),
        lax.all_gather(cotangent, "tensor", axis=1, tiled=True),
    )
    token_blocks = x_full.reshape(token_count, blocks_wide, block)
    cot_blocks = dy_full.reshape(token_count, blocks_wide, block)
    w_up = up_blocks[0]
    w_down = down_blocks[0]
    up_pos = kept_positions(up_mask, kept_up)
    up_rows = up_pos // strip_size
    up_cols = up_pos % strip_size
    token_chosen = jnp.take(token_blocks, up_rows, axis=1)
    product = jnp.einsum("nkb,kbc->nkc", token_chosen, w_up, preferred_element_type=jnp.float32)
    up_val = jnp.einsum("nkc,ks->nsc", product, one_hot(up_cols, strip_size), precision=highest)
    gate_val = gate_pre.reshape(token_count, strip_size, block).astype(jnp.float32)
    sigmoid_gate = jax.nn.sigmoid(gate_val)
    activated = gate_val * sigmoid_gate
    hidden = (activated * up_val).astype(jnp.bfloat16).reshape(token_count, strip_size * block)
    my_rows = kept_positions(down_owner == position, strip_size)
    owned_mask = jnp.take(down_mask, my_rows, axis=0)
    down_pos = kept_positions(owned_mask, kept_down)
    slots = down_pos // blocks_wide
    down_cols = down_pos % blocks_wide
    empty = jnp.zeros((token_count, strip_size, block), jnp.bfloat16)
    hidden_owned = picker(
        my_rows, block, empty, lax.all_gather(hidden, "tensor", axis=1, tiled=True)
    )
    h_chosen = jnp.take(hidden_owned, slots, axis=1)
    product = jnp.einsum("nkb,kbc->nkc", h_chosen, w_down, preferred_element_type=jnp.float32)
    out_part = jnp.einsum(
        "nkc,kj->njc", product, one_hot(down_cols, blocks_wide), precision=highest
    )
    out_part = out_part.astype(jnp.bfloat16).reshape(1, token_count, model_width)
    dy_chosen = jnp.take(cot_blocks, down_cols, axis=1)
    down_term = jnp.einsum("nkb,nkc->kbc", h_chosen, dy_chosen, preferred_element_type=jnp.float32)[
        None
    ]
    backward = jnp.einsum("nkc,kbc->nkb", dy_chosen, w_down, preferred_element_type=jnp.float32)
    dh_owned = jnp.einsum("nkb,ka->nab", backward, one_hot(slots, strip_size), precision=highest)
    dh_owned = dh_owned.astype(jnp.bfloat16).reshape(token_count, strip_size * block)
    home_index = down_owner * strip_size + row_slots(down_owner, devices)
    targets = position * strip_size + jnp.arange(strip_size, dtype=jnp.int32)
    wanted = jnp.take(home_index, targets)
    hidden_grad = picker(
        wanted, block, empty, lax.all_gather(dh_owned, "tensor", axis=1, tiled=True)
    )
    dh_float = hidden_grad.astype(jnp.float32)
    gate_grad = (dh_float * up_val * sigmoid_gate * (1.0 + gate_val * (1.0 - sigmoid_gate))).astype(
        jnp.bfloat16
    )
    gate_grad = gate_grad.reshape(token_count, strip_size * block)
    up_act_grad = (dh_float * activated).astype(jnp.bfloat16)
    du_chosen = jnp.take(up_act_grad, up_cols, axis=1)
    product = jnp.einsum("nkc,kbc->nkb", du_chosen, w_up, preferred_element_type=jnp.float32)
    in_part = jnp.einsum("nkb,kr->nrb", product, one_hot(up_rows, blocks_wide), precision=highest)
    in_part = in_part.astype(jnp.bfloat16).reshape(1, token_count, model_width)
    up_term = jnp.einsum(
        "nkb,nkc->kbc", token_chosen, du_chosen, preferred_element_type=jnp.float32
    )[None]
    out_pieces, in_pieces = (
        lax.all_to_all(out_part, "tensor", split_axis=2, concat_axis=0, tiled=True),
        lax.all_to_all(in_part, "tensor", split_axis=2, concat_axis=0, tiled=True),
    )
    mixed = jnp.sum(out_pieces.astype(jnp.float32), axis=0).astype(jnp.bfloat16)
    input_grad = jnp.sum(in_pieces.astype(jnp.float32), axis=0).astype(jnp.bfloat16)
    up_sum, down_sum = (
        lax.psum_scatter(
            up_term.astype(jnp.bfloat16), "dp", scatter_dimension=1, tiled=True
        ).astype(jnp.float32),
        lax.psum_scatter(
            down_term.astype(jnp.bfloat16), "dp", scatter_dimension=1, tiled=True
        ).astype(jnp.float32),
    )
    up_grad = up_sum.astype(jnp.bfloat16)
    down_grad = down_sum.astype(jnp.bfloat16)
    return (mixed, input_grad, gate_grad, up_grad, down_grad)


def solution(mesh):
    placed = (
        P("dp", "tensor"),
        P("dp", "tensor"),
        P("tensor", None, None, None),
        P(None, "tensor"),
        P("tensor", None, None, None),
        P(),
        P(),
        P("dp", "tensor"),
    )
    return jax.shard_map(
        shards,
        mesh=mesh,
        in_specs=placed,
        out_specs=(
            P("dp", "tensor"),
            P("dp", "tensor"),
            P("dp", "tensor"),
            P("tensor", "dp", None, None),
            P("tensor", "dp", None, None),
        ),
        check_vma=False,
    )
```

profile of v0, /device:TPU:2, one launch (start us, length us, event | category | flops | bytes accessed | tf_op | source)
XLA Modules:
  0.0 517.0 jit_solution(11576796951660111175)
XLA Ops:
  7.2 1.6 copy.130
  8.9 1.5 copy.121
  10.5 0.7 fusion.58
  12.4 0.8 select_reduce_fusion
  14.0 1.0 scatter_custom_fusion
  14.9 0.8 copy.115
  17.3 1.0 scatter_custom_fusion.1
  18.4 79.6 %all-gather.9.cloned.1.call-done = bf16[128,4096]{0,1:T(8,128)(2,1)} async-done(((bf16[128,128]{0,1:T(8,128)(2,1)}), bf16[128,4096]{0,1:T(8,128)(2,1)}) %all-gather.9.cloned.1.call-update) | async-done | bytes 1048592 | tf_op jit(solution)/shard_map/all_gather | solution.py:46
  98.0 1.6 copy.131
  99.6 2.2 gather_fusion.5
  101.8 3.8 convolution_bitcast_fusion.1
  105.7 3.8 fusion.48
  109.5 0.8 copy.146
  111.6 1.4 scatter_custom_fusion.2
  115.2 66.1 %all-gather.5.cloned.1.call-done = bf16[128,4096]{0,1:T(8,128)(2,1)} async-done(((bf16[128,128]{0,1:T(8,128)(2,1)}), bf16[128,4096]{0,1:T(8,128)(2,1)}) %all-gather.5.cloned.1.call-update) | async-done | bytes 1048592 | tf_op jit(solution)/shard_map/all_gather | solution.py:45
  181.2 1.6 copy.122
  182.9 2.2 gather_fusion.2
  185.0 4.3 convolution_bitcast_fusion.3
  189.4 80.9 %all-gather.11.cloned.1.call-done = bf16[128,16384]{0,1:T(8,128)(2,1)} async-done(((bf16[128,512]{0,1:T(8,128)(2,1)}), bf16[128,16384]{0,1:T(8,128)(2,1)}) %all-gather.11.cloned.1.call-update) | async-done | bytes 4194320 | tf_op jit(solution)/shard_map/all_gather | solution.py:88
  270.3 6.4 %copy.134 = bf16[128,128,128]{2,0,1:T(8,128)(2,1)} copy(bf16[128,128,128]{0,2,1:T(8,128)(2,1)} %bitcast.106) | data formatting | bytes 8388608 | tf_op jit(solution)/shard_map/reshape | solution.py:28
  276.7 2.8 gather_fusion.6
  279.4 6.0 %fusion.54 = (bf16[128,4,128]{2,1,0:T(4,128)(2,1)S(1)}, bf16[128,4,128]{2,1,0:T(4,128)(2,1)S(1)}, bf16[128,4,128]{2,1,0:T(4,128)(2,1)S(1)}) fusion(f32[128,4,128]{2,1,0:T(4,128)S(1)} %reshape.234, bf16[4,128,128]{2,1,0:T(8,128)(2,1)S(1)} %gather_fusion.6, pred[4]{0:T(512)(128)(4,1)S(1)} %copy-done.17, pred[4]{0:T(512)(128)(4,1)S(1)} %copy-done.16, ...), kind=kOutput, calls=%fused_computation.55 | convolution fusion | flops 51511552 | bytes 4981000 | tf_op jit(solution)/shard_map/nkc,ks->nsc/dot_general | solution.py:57
  285.5 0.8 copy.145
  286.4 2.2 gather_fusion.7
  288.6 4.6 convert_bitcast_fusion.1
  293.9 5.2 %convolution_bitcast_fusion = f32[128,64,128]{2,0,1:T(8,128)} fusion(bf16[1,64,128,128]{3,2,1,0:T(8,128)(2,1)S(1)} %copy-done, bf16[64,128,128]{2,1,0:T(8,128)(2,1)} %gather_fusion.7, pred[64]{0:T(512)(128)(4,1)S(1)} %copy-done.6), kind=kOutput, calls=%fused_computation.19 | convolution fusion | flops 269484032 | bytes 8388672 | tf_op jit(solution)/shard_map/nkc,kbc->nkb/dot_general | solution.py:97
  299.1 72.1 %all-gather.7.cloned.1.call-done = bf16[128,16384]{0,1:T(8,128)(2,1)} async-done(((bf16[128,512]{0,1:T(8,128)(2,1)}), bf16[128,16384]{0,1:T(8,128)(2,1)}) %all-gather.7.cloned.1.call-update) | async-done | bytes 4194320 | tf_op jit(solution)/shard_map/all_gather | solution.py:69
  371.2 6.5 %copy.125 = bf16[128,128,128]{2,0,1:T(8,128)(2,1)} copy(bf16[128,128,128]{0,2,1:T(8,128)(2,1)} %bitcast.107) | data formatting | bytes 8388608 | tf_op jit(solution)/shard_map/reshape | solution.py:28
  377.7 2.8 gather_fusion.3
  380.6 2.1 gather_fusion.4
  382.8 4.6 convert_bitcast_fusion
  387.9 6.1 %fusion.36 = bf16[128,32,128]{2,1,0:T(8,128)(2,1)S(1)} fusion(f32[128,64,128]{2,0,1:T(8,128)} %convolution_bitcast_fusion, s32[64]{0:T(128)S(1)} %copy-done.14), kind=kOutput, calls=%fused_computation.45 | convolution fusion | flops 403179520 | bytes 5243136 | tf_op jit(solution)/shard_map/nkb,kr->nrb/dot_general | solution.py:98
  394.5 2.8 copy.138
  397.9 22.4 %reduce.15 = bf16[4096,128]{1,0:T(8,128)(2,1)S(1)} reduce(bf16[4096,1,128]{2,1,0:T(2,128)(2,1)S(1)} %bitcast.102, bf16[]{:T(256)} %broadcast.484), dimensions={1}, to_apply=%bitcast.95.reduce_sub_computation | reduce | bytes 2097154
  420.3 1.1 reshape.359
  421.4 7.0 %all-to-all-start.1 = ((bf16[32,2,8192]{2,1,0:T(2,128)(2,1)}), bf16[32,2,8192]{2,1,0:T(2,128)(2,1)S(1)}, u32[]{:S(2)}, u32[]{:S(2)}) async-start(bf16[32,2,8192]{2,1,0:T(2,128)(2,1)} %reshape.359), calls=%async_computation.1 | async-start | bytes 2097152 | tf_op jit(solution)/shard_map/all_to_all | solution.py:105
  428.4 2.4 convolution_bitcast_fusion.2
  430.8 4.1 fusion.39
  434.9 1.3 reshape.228
  436.2 5.0 copy.129
  441.2 23.4 %reduce.14 = bf16[4096,128]{1,0:T(8,128)(2,1)} reduce(bf16[4096,1,128]{2,1,0:T(2,128)(2,1)S(1)} %bitcast.103, bf16[]{:T(256)} %broadcast.484), dimensions={1}, to_apply=%bitcast.93.reduce_sub_computation | reduce | bytes 2097154
  464.6 2.1 reshape.357
  466.7 9.8 %all-to-all-start = ((bf16[32,2,8192]{2,1,0:T(2,128)(2,1)}), bf16[32,2,8192]{2,1,0:T(2,128)(2,1)}, u32[]{:S(2)}, u32[]{:S(2)}) async-start(bf16[32,2,8192]{2,1,0:T(2,128)(2,1)} %reshape.357), calls=%async_computation | async-start | bytes 2097152 | tf_op jit(solution)/shard_map/all_to_all | solution.py:104
  477.3 1.0 reshape.360
  478.6 0.7 copy.142
  479.3 22.0 %all-to-all-done = bf16[32,2,8192]{2,1,0:T(2,128)(2,1)} async-done(((bf16[32,2,8192]{2,1,0:T(2,128)(2,1)}), bf16[32,2,8192]{2,1,0:T(2,128)(2,1)}, u32[]{:S(2)}, u32[]{:S(2)}) %all-to-all-start) | async-done | bytes 1048608 | tf_op jit(solution)/shard_map/all_to_all | solution.py:104
  501.3 5.8 %reshape.358 = bf16[4096,1,128]{2,1,0:T(2,128)(2,1)} reshape(bf16[32,2,8192]{2,1,0:T(2,128)(2,1)} %all-to-all-done) | data formatting | bytes 2097152
  507.1 1.9 copy.147
  (100 shorter events, 11.4 us)
Async XLA Ops:
  7.2 177.9 %copy-start = (bf16[1,64,128,128]{3,2,1,0:T(8,128)(2,1)S(1)}, bf16[1,64,128,128]{3,2,1,0:T(8,128)(2,1)}, u32[]{:S(2)}) copy-start(bf16[1,64,128,128]{3,2,1,0:T(8,128)(2,1)} %param.16) | copy-start | bytes 6291460
  7.2 90.8 %all-gather.9.cloned.1.call-start = ((), (), s32[]{:S(2)}) async-start(), calls=%async_computation.6 | async-start | bytes 1081344 | tf_op jit(solution)/shard_map/all_gather | solution.py:46
  8.9 172.4 %all-gather.5.cloned.1.call-start = ((), (), s32[]{:S(2)}) async-start(), calls=%async_computation.4 | async-start | bytes 1081344 | tf_op jit(solution)/shard_map/all_gather | solution.py:45
  10.4 259.9 %all-gather.11.cloned.1.call-start = ((), (), s32[]{:S(2)}) async-start(), calls=%async_computation.7 | async-start | bytes 4325376 | tf_op jit(solution)/shard_map/all_gather | solution.py:88
  18.3 83.5 %copy-start.11 = (s32[64]{0:T(128)}, s32[64]{0:T(128)S(1)}, u32[]{:S(2)}) copy-start(s32[64]{0:T(128)S(1)} %get-tuple-element.20) | copy-start | bytes 772
  18.3 87.3 %copy-start.4 = (s32[64]{0:T(128)}, s32[64]{0:T(128)S(1)}, u32[]{:S(2)}) copy-start(s32[64]{0:T(128)S(1)} %get-tuple-element.33) | copy-start | bytes 772
  105.6 4.7 copy-start.9
  105.7 5.0 copy-start.3
  110.3 260.9 %all-gather.7.cloned.1.call-start = ((), (), s32[]{:S(2)}) async-start(), calls=%async_computation.5 | async-start | bytes 4325376 | tf_op jit(solution)/shard_map/all_gather | solution.py:69
  114.6 0.5 copy-start.13
  114.6 70.4 %copy-start.7 = (pred[64]{0:T(512)(128)(4,1)}, pred[64]{0:T(512)(128)(4,1)S(1)}, u32[]{:S(2)}) copy-start(pred[64]{0:T(512)(128)(4,1)S(1)} %get-tuple-element.38) | copy-start | bytes 196
  270.3 9.2 %copy-start.15 = (s32[64]{0:T(128)S(1)}, s32[64]{0:T(128)}, u32[]{:S(2)}) copy-start(s32[64]{0:T(128)} %get-tuple-element.14) | copy-start | bytes 772
  270.3 9.2 %copy-start.16 = (pred[4]{0:T(512)(128)(4,1)S(1)}, pred[4]{0:T(512)(128)(4,1)}, u32[]{:S(2)}) copy-start(pred[4]{0:T(512)(128)(4,1)} %get-tuple-element.15) | copy-start | bytes 16
  270.3 9.2 %copy-start.17 = (pred[4]{0:T(512)(128)(4,1)S(1)}, pred[4]{0:T(512)(128)(4,1)}, u32[]{:S(2)}) copy-start(pred[4]{0:T(512)(128)(4,1)} %get-tuple-element.17) | copy-start | bytes 16
  286.3 223.6 %reduce-scatter.3.cloned.1.call-start = ((), (), s32[]{:S(2)}) async-start(), calls=%async_computation.8 | async-start | bytes 2228224 | tf_op jit(solution)/shard_map/reduce_scatter | solution.py:110
  286.4 2.2 copy-start.6
  286.4 2.2 copy-start.8
  293.2 0.7 copy-start.10
  293.2 0.7 copy-start.5
  293.2 216.7 %reduce-scatter.5.cloned.1.call-start = ((), (), s32[]{:S(2)}) async-start(), calls=%async_computation.9 | async-start | bytes 2228224 | tf_op jit(solution)/shard_map/reduce_scatter | solution.py:113
  387.3 0.6 copy-start.14
  420.2 8.2 %copy-start.2 = (bf16[64,128,128]{2,1,0:T(8,128)(2,1)S(1)}, bf16[64,128,128]{2,1,0:T(8,128)(2,1)}, u32[]{:S(2)}) copy-start(bf16[64,128,128]{2,1,0:T(8,128)(2,1)} %gather_fusion.4) | copy-start | bytes 6291460
  421.4 45.4 %all-to-all-start.1 = ((bf16[32,2,8192]{2,1,0:T(2,128)(2,1)}), bf16[32,2,8192]{2,1,0:T(2,128)(2,1)S(1)}, u32[]{:S(2)}, u32[]{:S(2)}) async-start(bf16[32,2,8192]{2,1,0:T(2,128)(2,1)} %reshape.359), calls=%async_computation.1 | async-start | bytes 2097152 | tf_op jit(solution)/shard_map/all_to_all | solution.py:105
  428.4 2.4 copy-start.12
  466.7 34.6 %all-to-all-start = ((bf16[32,2,8192]{2,1,0:T(2,128)(2,1)}), bf16[32,2,8192]{2,1,0:T(2,128)(2,1)}, u32[]{:S(2)}, u32[]{:S(2)}) async-start(bf16[32,2,8192]{2,1,0:T(2,128)(2,1)} %reshape.357), calls=%async_computation | async-start | bytes 2097152 | tf_op jit(solution)/shard_map/all_to_all | solution.py:104
  507.1 2.8 copy-start.1
Sparse Core Ops, SparseCore 0:
  11.8 86.1 all-gather.8
  101.7 79.5 all-gather.4
  185.0 85.2 all-gather.10
  286.4 84.7 all-gather.6
  374.4 59.0 reduce-scatter.2
  436.8 61.4 reduce-scatter.4
where the time goes:
time: 525 us; the launch traced here: 517 us
  waiting for transfers between devices  321 us (61%)
  local copies, waits for them, and re-layouts  67 us (13%)
  other arithmetic  52.4 us (10%)
  matrix products  44.8 us (9%)
  starting transfers between devices  17.1 us (3%)
  between operations  14.8 us (3%)
    all_gather x1, waiting for transfers between devices, shards(): lax.all_gather(dh_owned, 'tensor', axis=1, tiled=True)  80.9 us
    all_gather x1, waiting for transfers between devices, shards(): lax.all_gather(cotangent, 'tensor', axis=1, tiled=True)  79.6 us
    all_gather x1, waiting for transfers between devices, shards(): lax.all_gather(hidden, 'tensor', axis=1, tiled=True)  72.1 us
    all_gather x1, waiting for transfers between devices, shards(): lax.all_gather(tokens, 'tensor', axis=1, tiled=True)  66.1 us
    unnamed x2, other arithmetic  45.8 us
    all_to_all x1, waiting for transfers between devices, shards(): lax.all_to_all(out_part, 'tensor', split_axis=2, concat_axis=0, tiled=True)  22 us
    unnamed x50, local copies, waits for them, and re-layouts  20.5 us
    reshape x2, local copies, waits for them, and re-layouts, picker(): shaped = segment.reshape(segment.shape[0], block_count, block)  12.9 us
  transfers between devices with their start and end apart: 8, of which 5 were waited for; matrix products, arithmetic and copies ran while one was open for 28% of the time, Pallas kernels for 0%

commit v1 on v0

--- a/solution.py
+++ b/solution.py
@@ -65,9 +65,16 @@
     slots = down_pos // blocks_wide
     down_cols = down_pos % blocks_wide
     empty = jnp.zeros((token_count, strip_size, block), jnp.bfloat16)
-    hidden_owned = picker(
-        my_rows, block, empty, lax.all_gather(hidden, "tensor", axis=1, tiled=True)
-    )
+
+    def _supply_streams(arr, along_axis, along_dim):
+        low = lax.axis_size(along_axis)
+        r1 = jnp.concatenate(low * [arr], along_dim)
+        big = lax.all_to_all(
+            r1, split_axis=along_dim, axis_name=along_axis, concat_axis=along_dim, tiled=True
+        )
+        return big
+
+    hidden_owned = picker(my_rows, block, empty, _supply_streams(hidden, "tensor", 1))
     h_chosen = jnp.take(hidden_owned, slots, axis=1)
     product = jnp.einsum("nkb,kbc->nkc", h_chosen, w_down, preferred_element_type=jnp.float32)
     out_part = jnp.einsum(

time: 525 us -> 540 us (1.029)
  waiting for transfers between devices: 321 us -> 329 us
  starting transfers between devices: 17.1 us -> 22.6 us
    all_to_all x0 -> x1, waiting for transfers between devices: none -> 80.1 us  [_supply_streams(): lax.all_to_all(r1, split_axis=along_dim, axis_name=along_axis, concat_axi...]
    all_gather x1 -> x0, waiting for transfers between devices: 72.1 us -> none  [shards(): lax.all_gather(hidden, 'tensor', axis=1, tiled=True)]
    all_to_all x0 -> x1, starting transfers between devices: none -> 6.71 us  [_supply_streams(): lax.all_to_all(r1, split_axis=along_dim, axis_name=along_axis, concat_axi...]
  transfers between devices with their start and end apart: 8 -> 8, of which waited for: 5 -> 5; matrix products, arithmetic and copies ran while one was open for 28% -> 27% of each run, Pallas kernels for 0% -> 0%
where the time goes in v1:
time: 540 us; the launch traced here: 532 us
  waiting for transfers between devices  329 us (61%)
  local copies, waits for them, and re-layouts  69.2 us (13%)
  other arithmetic  52.4 us (10%)
  matrix products  44.8 us (8%)
  starting transfers between devices  22.6 us (4%)
  between operations  14.5 us (3%)
    all_gather x1, waiting for transfers between devices, shards(): lax.all_gather(dh_owned, 'tensor', axis=1, tiled=True)  80.9 us
    all_to_all x1, waiting for transfers between devices, _supply_streams(): lax.all_to_all(r1, split_axis=along_dim, axis_name=along_axis, concat_axi...  80.1 us
    all_gather x1, waiting for transfers between devices, shards(): lax.all_gather(cotangent, 'tensor', axis=1, tiled=True)  79.6 us
    all_gather x1, waiting for transfers between devices, shards(): lax.all_gather(tokens, 'tensor', axis=1, tiled=True)  66.1 us
    unnamed x2, other arithmetic  45.8 us
    all_to_all x1, waiting for transfers between devices, shards(): lax.all_to_all(out_part, 'tensor', split_axis=2, concat_axis=0, tiled=True)  21.8 us
    unnamed x50, local copies, waits for them, and re-layouts  20.5 us
    reshape x2, local copies, waits for them, and re-layouts, picker(): shaped = segment.reshape(segment.shape[0], block_count, block)  12.9 us
  transfers between devices with their start and end apart: 8, of which 5 were waited for; matrix products, arithmetic and copies ran while one was open for 27% of the time, Pallas kernels for 0%

profile of v1, /device:TPU:2, one launch (start us, length us, event | category | flops | bytes accessed | tf_op | source)
XLA Modules:
  0.0 532.2 jit_solution(13104569155045284431)
XLA Ops:
  7.2 1.6 copy.130
  8.9 1.5 copy.121
  10.5 0.7 fusion.58
  12.4 0.8 select_reduce_fusion
  14.0 1.0 scatter_custom_fusion
  14.9 0.8 copy.115
  17.3 1.0 scatter_custom_fusion.1
  18.4 79.6 %all-gather.6.cloned.1.call-done = bf16[128,4096]{0,1:T(8,128)(2,1)} async-done(((bf16[128,128]{0,1:T(8,128)(2,1)}), bf16[128,4096]{0,1:T(8,128)(2,1)}) %all-gather.6.cloned.1.call-update) | async-done | bytes 1048592 | tf_op jit(solution)/shard_map/all_gather | solution.py:46
  98.0 1.6 copy.131
  99.6 2.2 gather_fusion.5
  101.8 3.8 convolution_bitcast_fusion.1
  105.7 3.8 fusion.48
  109.5 0.8 copy.146
  111.5 1.4 scatter_custom_fusion.2
  115.1 66.1 %all-gather.4.cloned.1.call-done = bf16[128,4096]{0,1:T(8,128)(2,1)} async-done(((bf16[128,128]{0,1:T(8,128)(2,1)}), bf16[128,4096]{0,1:T(8,128)(2,1)}) %all-gather.4.cloned.1.call-update) | async-done | bytes 1048592 | tf_op jit(solution)/shard_map/all_gather | solution.py:45
  181.2 1.6 copy.122
  182.9 2.2 gather_fusion.2
  185.0 4.3 convolution_bitcast_fusion.3
  189.4 80.9 %all-gather.8.cloned.1.call-done = bf16[128,16384]{0,1:T(8,128)(2,1)} async-done(((bf16[128,512]{0,1:T(8,128)(2,1)}), bf16[128,16384]{0,1:T(8,128)(2,1)}) %all-gather.8.cloned.1.call-update) | async-done | bytes 4194320 | tf_op jit(solution)/shard_map/all_gather | solution.py:95
  270.3 6.4 %copy.134 = bf16[128,128,128]{2,0,1:T(8,128)(2,1)} copy(bf16[128,128,128]{0,2,1:T(8,128)(2,1)} %bitcast.106) | data formatting | bytes 8388608 | tf_op jit(solution)/shard_map/reshape | solution.py:28
  276.7 2.8 gather_fusion.6
  279.4 6.0 %fusion.54 = (bf16[128,4,128]{2,1,0:T(4,128)(2,1)S(1)}, bf16[128,4,128]{2,1,0:T(4,128)(2,1)S(1)}, bf16[128,4,128]{2,1,0:T(4,128)(2,1)S(1)}) fusion(f32[128,4,128]{2,1,0:T(4,128)S(1)} %reshape.300, bf16[4,128,128]{2,1,0:T(8,128)(2,1)S(1)} %gather_fusion.6, pred[4]{0:T(512)(128)(4,1)S(1)} %copy-done.17, pred[4]{0:T(512)(128)(4,1)S(1)} %copy-done.16, ...), kind=kOutput, calls=%fused_computation.55 | convolution fusion | flops 51511552 | bytes 4981000 | tf_op jit(solution)/shard_map/nkc,ks->nsc/dot_general | solution.py:57
  285.6 2.9 concatenate.7
  288.6 6.7 %all-to-all-start = ((bf16[128,32,512]{0,2,1:T(8,128)(2,1)}), bf16[128,32,512]{0,2,1:T(8,128)(2,1)}, u32[]{:S(2)}, u32[]{:S(2)}) async-start(bf16[128,32,512]{0,2,1:T(8,128)(2,1)} %concatenate.7), calls=%async_computation | async-start | bytes 8388608 | tf_op jit(solution)/shard_map/all_to_all | solution.py:72
  295.4 2.1 gather_fusion.7
  297.5 4.6 convert_bitcast_fusion.1
  302.8 5.2 convolution_bitcast_fusion
  308.0 80.1 %all-to-all-done = bf16[128,32,512]{0,2,1:T(8,128)(2,1)} async-done(((bf16[128,32,512]{0,2,1:T(8,128)(2,1)}), bf16[128,32,512]{0,2,1:T(8,128)(2,1)}, u32[]{:S(2)}, u32[]{:S(2)}) %all-to-all-start) | async-done | bytes 4194336 | tf_op jit(solution)/shard_map/all_to_all | solution.py:72
  388.1 6.5 %copy.125 = bf16[128,128,128]{2,0,1:T(8,128)(2,1)} copy(bf16[128,128,128]{0,2,1:T(8,128)(2,1)} %bitcast.9) | data formatting | bytes 8388608 | tf_op jit(solution)/shard_map/reshape | solution.py:28
  394.6 2.8 gather_fusion.3
  397.5 2.1 gather_fusion.4
  399.6 4.6 convert_bitcast_fusion
  404.8 6.1 %fusion.36 = bf16[128,32,128]{2,1,0:T(8,128)(2,1)S(1)} fusion(f32[128,64,128]{2,0,1:T(8,128)} %convolution_bitcast_fusion, s32[64]{0:T(128)S(1)} %copy-done.14), kind=kOutput, calls=%fused_computation.45 | convolution fusion | flops 403179520 | bytes 5243136 | tf_op jit(solution)/shard_map/nkb,kr->nrb/dot_general | solution.py:105
  411.4 2.8 copy.138
  414.7 22.4 %reduce.15 = bf16[4096,128]{1,0:T(8,128)(2,1)S(1)} reduce(bf16[4096,1,128]{2,1,0:T(2,128)(2,1)S(1)} %bitcast.102, bf16[]{:T(256)} %broadcast.485), dimensions={1}, to_apply=%bitcast.95.reduce_sub_computation | reduce | bytes 2097154
  437.2 1.1 reshape.425
  438.3 5.9 %all-to-all-start.2 = ((bf16[32,2,8192]{2,1,0:T(2,128)(2,1)}), bf16[32,2,8192]{2,1,0:T(2,128)(2,1)S(1)}, u32[]{:S(2)}, u32[]{:S(2)}) async-start(bf16[32,2,8192]{2,1,0:T(2,128)(2,1)} %reshape.425), calls=%async_computation.2 | async-start | bytes 2097152 | tf_op jit(solution)/shard_map/all_to_all | solution.py:112
  444.2 2.4 convolution_bitcast_fusion.2
  446.6 4.1 fusion.39
  450.6 1.3 reshape.294
  451.9 5.0 copy.129
  457.0 23.4 %reduce.14 = bf16[4096,128]{1,0:T(8,128)(2,1)} reduce(bf16[4096,1,128]{2,1,0:T(2,128)(2,1)S(1)} %bitcast.103, bf16[]{:T(256)} %broadcast.485), dimensions={1}, to_apply=%bitcast.93.reduce_sub_computation | reduce | bytes 2097154
  480.3 2.1 reshape.423
  482.5 9.8 %all-to-all-start.1 = ((bf16[32,2,8192]{2,1,0:T(2,128)(2,1)}), bf16[32,2,8192]{2,1,0:T(2,128)(2,1)}, u32[]{:S(2)}, u32[]{:S(2)}) async-start(bf16[32,2,8192]{2,1,0:T(2,128)(2,1)} %reshape.423), calls=%async_computation.1 | async-start | bytes 2097152 | tf_op jit(solution)/shard_map/all_to_all | solution.py:111
  493.0 1.0 reshape.426
  495.1 21.8 %all-to-all-done.1 = bf16[32,2,8192]{2,1,0:T(2,128)(2,1)} async-done(((bf16[32,2,8192]{2,1,0:T(2,128)(2,1)}), bf16[32,2,8192]{2,1,0:T(2,128)(2,1)}, u32[]{:S(2)}, u32[]{:S(2)}) %all-to-all-start.1) | async-done | bytes 1048608 | tf_op jit(solution)/shard_map/all_to_all | solution.py:111
  516.8 5.8 %reshape.424 = bf16[4096,1,128]{2,1,0:T(2,128)(2,1)} reshape(bf16[32,2,8192]{2,1,0:T(2,128)(2,1)} %all-to-all-done.1) | data formatting | bytes 2097152
  522.6 1.9 copy.147
  (100 shorter events, 12.3 us)
Async XLA Ops:
  7.2 177.9 %copy-start = (bf16[1,64,128,128]{3,2,1,0:T(8,128)(2,1)S(1)}, bf16[1,64,128,128]{3,2,1,0:T(8,128)(2,1)}, u32[]{:S(2)}) copy-start(bf16[1,64,128,128]{3,2,1,0:T(8,128)(2,1)} %param.16) | copy-start | bytes 6291460
  7.2 90.8 %all-gather.6.cloned.1.call-start = ((), (), s32[]{:S(2)}) async-start(), calls=%async_computation.6 | async-start | bytes 1081344 | tf_op jit(solution)/shard_map/all_gather | solution.py:46
  8.9 172.4 %all-gather.4.cloned.1.call-start = ((), (), s32[]{:S(2)}) async-start(), calls=%async_computation.5 | async-start | bytes 1081344 | tf_op jit(solution)/shard_map/all_gather | solution.py:45
  10.4 259.9 %all-gather.8.cloned.1.call-start = ((), (), s32[]{:S(2)}) async-start(), calls=%async_computation.7 | async-start | bytes 4325376 | tf_op jit(solution)/shard_map/all_gather | solution.py:95
  18.3 83.5 %copy-start.11 = (s32[64]{0:T(128)}, s32[64]{0:T(128)S(1)}, u32[]{:S(2)}) copy-start(s32[64]{0:T(128)S(1)} %get-tuple-element.20) | copy-start | bytes 772
  18.3 87.3 %copy-start.4 = (s32[64]{0:T(128)}, s32[64]{0:T(128)S(1)}, u32[]{:S(2)}) copy-start(s32[64]{0:T(128)S(1)} %get-tuple-element.33) | copy-start | bytes 772
  105.6 4.6 copy-start.9
  105.7 5.0 copy-start.3
  114.6 0.5 copy-start.13
  114.6 70.4 %copy-start.7 = (pred[64]{0:T(512)(128)(4,1)}, pred[64]{0:T(512)(128)(4,1)S(1)}, u32[]{:S(2)}) copy-start(pred[64]{0:T(512)(128)(4,1)S(1)} %get-tuple-element.38) | copy-start | bytes 196
  270.3 9.2 %copy-start.15 = (s32[64]{0:T(128)S(1)}, s32[64]{0:T(128)}, u32[]{:S(2)}) copy-start(s32[64]{0:T(128)} %get-tuple-element.14) | copy-start | bytes 772
  270.3 9.2 %copy-start.16 = (pred[4]{0:T(512)(128)(4,1)S(1)}, pred[4]{0:T(512)(128)(4,1)}, u32[]{:S(2)}) copy-start(pred[4]{0:T(512)(128)(4,1)} %get-tuple-element.15) | copy-start | bytes 16
  270.3 9.2 %copy-start.17 = (pred[4]{0:T(512)(128)(4,1)S(1)}, pred[4]{0:T(512)(128)(4,1)}, u32[]{:S(2)}) copy-start(pred[4]{0:T(512)(128)(4,1)} %get-tuple-element.17) | copy-start | bytes 16
  288.6 99.5 %all-to-all-start = ((bf16[128,32,512]{0,2,1:T(8,128)(2,1)}), bf16[128,32,512]{0,2,1:T(8,128)(2,1)}, u32[]{:S(2)}, u32[]{:S(2)}) async-start(bf16[128,32,512]{0,2,1:T(8,128)(2,1)} %concatenate.7), calls=%async_computation | async-start | bytes 8388608 | tf_op jit(solution)/shard_map/all_to_all | solution.py:72
  295.3 230.1 %reduce-scatter.3.cloned.1.call-start = ((), (), s32[]{:S(2)}) async-start(), calls=%async_computation.8 | async-start | bytes 2228224 | tf_op jit(solution)/shard_map/reduce_scatter | solution.py:117
  295.4 2.1 copy-start.6
  295.4 2.1 copy-start.8
  302.1 0.7 copy-start.10
  302.1 0.7 copy-start.5
  302.1 223.3 %reduce-scatter.5.cloned.1.call-start = ((), (), s32[]{:S(2)}) async-start(), calls=%async_computation.9 | async-start | bytes 2228224 | tf_op jit(solution)/shard_map/reduce_scatter | solution.py:120
  404.2 0.6 copy-start.14
  437.1 7.0 %copy-start.2 = (bf16[64,128,128]{2,1,0:T(8,128)(2,1)S(1)}, bf16[64,128,128]{2,1,0:T(8,128)(2,1)}, u32[]{:S(2)}) copy-start(bf16[64,128,128]{2,1,0:T(8,128)(2,1)} %gather_fusion.4) | copy-start | bytes 6291460
  438.3 44.2 %all-to-all-start.2 = ((bf16[32,2,8192]{2,1,0:T(2,128)(2,1)}), bf16[32,2,8192]{2,1,0:T(2,128)(2,1)S(1)}, u32[]{:S(2)}, u32[]{:S(2)}) async-start(bf16[32,2,8192]{2,1,0:T(2,128)(2,1)} %reshape.425), calls=%async_computation.2 | async-start | bytes 2097152 | tf_op jit(solution)/shard_map/all_to_all | solution.py:112
  444.2 2.4 copy-start.12
  482.5 34.4 %all-to-all-start.1 = ((bf16[32,2,8192]{2,1,0:T(2,128)(2,1)}), bf16[32,2,8192]{2,1,0:T(2,128)(2,1)}, u32[]{:S(2)}, u32[]{:S(2)}) async-start(bf16[32,2,8192]{2,1,0:T(2,128)(2,1)} %reshape.423), calls=%async_computation.1 | async-start | bytes 2097152 | tf_op jit(solution)/shard_map/all_to_all | solution.py:111
  522.6 2.8 copy-start.1
Sparse Core Ops, SparseCore 0:
  11.8 86.1 all-gather.5
  101.7 79.5 all-gather.3
  185.0 85.2 all-gather.7
  302.2 64.3 reduce-scatter.2
  404.4 58.2 reduce-scatter.4
